TPU v7x, 512 devices: a whole 4x4x16 slice. The times are simulated.
512 devices in a mesh: dom: 32 (over x, y, core), cls: 16 (over z).
Axes of the slice: x: 4, y: 4, z: 16, core: 2. Of those that a mesh axis runs over, the one named last changes fastest.
Arguments:
- images: bfloat16 [16384, 128, 128], P(('dom', 'cls')), may hold values from -6 to 6
- class_ids: int32 [16384], P(('dom', 'cls')), may hold values from 0 to 255, as said below
- shifts: int32 [16384, 2], P(('dom', 'cls')), may hold values from -16 to 16
- defocus_bins: int32 [16384], P(('dom', 'cls')), may hold values from 0 to 31
- defocus: float32 [32], replicated, may hold values from 20 to 200
- regular: float32 [128, 128], replicated, may hold values from 1 to 32
Outputs:
- class_avg: float32 [256, 128, 128], P('cls')
Inputs may be any that keep to these rules, and one draw needn't show every extreme that they name: `class_ids`: the owner of class k is k // 16. Among the 32 particles of one device exactly 8 have classes of one owner, and every other owner has at most 2 of them, exactly 2 for some; all devices with the same dom index have that same most loaded owner.
All inputs are finite; a program needn't handle non-finite values.
Results may differ from a plain program's by a relative error of at most 0.0055.
Values may be sent and summed in bfloat16 or wider, within the bound.
No kernel may reach another device: no remote copies, remote signals or barrier semaphores. Data moves between devices by JAX's collectives and lax.ppermute only.
A program may use at most 64 MiB of HBM per device.

v0:
```python
import math
import jax
import jax.numpy as jnp
from jax import lax
from jax.sharding import PartitionSpec as P

OWNED = 16
PHASE = 0.1
EPSILON = 1e-05


def hartley_tables(image_side):
    indices = jnp.arange(image_side, dtype=jnp.int32)
    product = indices[:, None] * indices[None, :] % image_side
    angles = product.astype(jnp.float32) * (2.0 * math.pi / image_side)
    return (jnp.cos(angles), jnp.sin(angles))


def frequency_squared(image_side):
    indices = jnp.arange(image_side, dtype=jnp.int32)
    signed = (
        jnp.where(indices < image_side // 2, indices, indices - image_side).astype(jnp.float32)
        / image_side
    )
    return signed[:, None] * signed[:, None] + signed[None, :] * signed[None, :]


def lookup(bins, defocus):
    levels = jnp.arange(defocus.shape[0], dtype=jnp.int32)
    return jnp.sum(jnp.where(bins[:, None] == levels[None, :], defocus[None, :], 0.0), axis=1)


def weigh(pictures, offsets, bins, defocus):
    count_rows = pictures.shape[0]
    image_side = pictures.shape[1]
    indices = jnp.arange(image_side, dtype=jnp.int32)
    source_rows = (indices[None, :] - offsets[:, 0:1]) % image_side
    source_cols = (indices[None, :] - offsets[:, 1:2]) % image_side
    row_select = (source_rows[:, :, None] == indices[None, None, :]).astype(jnp.bfloat16)
    col_select = (source_cols[:, :, None] == indices[None, None, :]).astype(jnp.bfloat16)
    shifted = jnp.einsum(
        "pij,pjk->pik", row_select, pictures, preferred_element_type=jnp.float32
    ).astype(jnp.bfloat16)
    shifted = jnp.einsum(
        "pik,plk->pil", shifted, col_select, preferred_element_type=jnp.float32
    ).astype(jnp.bfloat16)
    cosine, sine_table = hartley_tables(image_side)
    factor = 1.0 / math.sqrt(image_side)
    right_table = (
        jnp.concatenate([cosine + sine_table, cosine - sine_table], axis=1) * factor
    ).astype(jnp.bfloat16)
    left_table = (jnp.stack([cosine, sine_table]) * factor).astype(jnp.bfloat16)
    halves = jnp.dot(
        shifted.reshape(count_rows * image_side, image_side),
        right_table,
        preferred_element_type=jnp.float32,
    ).astype(jnp.bfloat16)
    halves = halves.reshape(count_rows, image_side, 2, image_side)
    spectrum = jnp.einsum("kux,pxkv->puv", left_table, halves, preferred_element_type=jnp.float32)
    ctf_values = -jnp.sin(
        lookup(bins, defocus)[:, None, None] * frequency_squared(image_side)[None] + PHASE
    )
    return (ctf_values * spectrum).astype(jnp.bfloat16).reshape(count_rows, image_side * image_side)


def body(images, class_ids, shifts, defocus_bins, defocus, regular):
    owners = lax.axis_size("cls")
    count_local = images.shape[0]
    image_side = images.shape[1]
    pixels = image_side * image_side
    capacity = min(4 * count_local // owners, count_local // 2)
    owner_of = class_ids // OWNED
    local_class = class_ids % OWNED
    member = (owner_of[:, None] == jnp.arange(owners, dtype=jnp.int32)[None, :]).astype(jnp.int32)
    before = jnp.cumsum(member, axis=0) - member
    ranked = jnp.sum(before * member, axis=1)
    slot_width = (count_local - capacity + owners - 2) // (owners - 1)
    slot_count = owners * slot_width
    target = jnp.where(ranked < slot_width, owner_of * slot_width + ranked, -1)
    matches = jnp.arange(slot_count, dtype=jnp.int32)[:, None] == target[None, :]
    filled = jnp.any(matches, axis=1)
    dispatch = matches.astype(jnp.bfloat16)

    def select_ints(selection, values):
        return jnp.sum(jnp.where(selection, values[None, :], 0), axis=1)

    slot_class = jnp.where(filled, select_ints(matches, local_class), OWNED)
    slot_bin = select_ints(matches, defocus_bins)
    payload = weigh(images, shifts, defocus_bins, defocus)
    outgoing = jnp.dot(dispatch, payload, preferred_element_type=jnp.float32).astype(jnp.bfloat16)
    outgoing = outgoing.reshape(owners, slot_width, pixels)
    labels = jnp.stack([slot_class, slot_bin], axis=1).reshape(owners, slot_width, 2)
    arrived, arrived_labels = (
        lax.all_to_all(outgoing, "cls", split_axis=0, concat_axis=0, tiled=True),
        lax.all_to_all(labels, "cls", split_axis=0, concat_axis=0, tiled=True),
    )
    arrived_rows = arrived.reshape(slot_count, pixels)
    arrived_tags = arrived_labels.reshape(slot_count, 2)
    surplus = capacity - slot_width
    extra_matches = (
        jnp.arange(surplus, dtype=jnp.int32)[:, None]
        == jnp.where(ranked >= slot_width, ranked - slot_width, -1)[None, :]
    )
    extra_filled = jnp.any(extra_matches, axis=1)
    extra_rows = jnp.dot(
        extra_matches.astype(jnp.bfloat16), payload, preferred_element_type=jnp.float32
    ).astype(jnp.bfloat16)
    extra_tags = jnp.stack(
        [
            select_ints(extra_matches, local_class),
            select_ints(extra_matches, defocus_bins),
            select_ints(extra_matches, shifts[:, 0]),
            select_ints(extra_matches, shifts[:, 1]),
            jnp.where(extra_filled, select_ints(extra_matches, owner_of), -1),
        ],
        axis=1,
    )
    gathered_rows, gathered_tags = (
        lax.all_gather(extra_rows, "cls", axis=0, tiled=True),
        lax.all_gather(extra_tags, "cls", axis=0, tiled=True),
    )
    mine = gathered_tags[:, 4] == lax.axis_index("cls")
    kept_class = jnp.where(mine, gathered_tags[:, 0], OWNED)
    arrived_rows = jnp.concatenate([arrived_rows, gathered_rows], axis=0)
    arrived_tags = jnp.concatenate(
        [arrived_tags, jnp.stack([kept_class, gathered_tags[:, 1]], axis=1)], axis=0
    )
    bin_count = defocus.shape[0]
    class_select = (jnp.arange(OWNED, dtype=jnp.int32)[:, None] == arrived_tags[None, :, 0]).astype(
        jnp.bfloat16
    )
    bin_select = (arrived_tags[:, 1:2] == jnp.arange(bin_count, dtype=jnp.int32)[None, :]).astype(
        jnp.bfloat16
    )
    numerator = jnp.dot(class_select, arrived_rows, preferred_element_type=jnp.float32)
    counts = jnp.dot(class_select, bin_select, preferred_element_type=jnp.float32)
    squared = frequency_squared(image_side).reshape(pixels)
    ctf_table = jnp.sin(defocus[:, None] * squared[None, :] + PHASE)
    ctf_table = ctf_table * ctf_table
    denominator = jnp.dot(counts, ctf_table, precision=lax.Precision.HIGHEST)
    numerator, denominator = lax.psum((numerator, denominator), "dom")
    average = numerator / (denominator + regular.reshape(1, pixels))
    cosine, sine_table = hartley_tables(image_side)
    right_table = jnp.concatenate([cosine + sine_table, cosine - sine_table], axis=1)
    left_table = jnp.stack([cosine, sine_table])
    halves = jnp.dot(
        average.reshape(OWNED * image_side, image_side),
        right_table,
        precision=lax.Precision.HIGHEST,
    )
    halves = halves.reshape(OWNED, image_side, 2, image_side)
    real_image = jnp.einsum("kux,pxkv->puv", left_table, halves, precision=lax.Precision.HIGHEST)
    power_mean = jnp.mean(real_image * real_image, axis=(1, 2), keepdims=True)
    return real_image / jnp.sqrt(power_mean + EPSILON)


def solution(mesh):
    in_specs = (
        P(("dom", "cls"), None, None),
        P(("dom", "cls")),
        P(("dom", "cls"), None),
        P(("dom", "cls")),
        P(),
        P(),
    )
    out_specs = P("cls", None, None)
    return jax.shard_map(body, mesh=mesh, in_specs=in_specs, out_specs=out_specs, check_vma=False)
```

profile of v0, /device:TPU:6, one launch (start us, length us, event | category | flops | bytes accessed | tf_op | source)
XLA Modules:
  0.0 312.1 jit_solution(7579158338892761363)
XLA Ops:
  7.1 0.7 and_select_fusion
  8.1 0.8 slice_bitcast_fusion.3
  9.0 2.4 fusion.15
  11.4 1.9 convolution_convert_fusion.2
  13.4 2.1 reshape.289
  15.8 9.2 %fusion.5 = bf16[32,128,128]{1,2,0:T(8,128)(2,1)S(1)} fusion(bf16[32,128,2,128]{3,2,1,0:T(2,128)(2,1)} %reshape.289, f32[128,128]{0,1:T(8,128)S(1)} %copy.34, f32[32]{0:T(128)S(1)} %select_reduce_fusion, f32[1,128,128]{2,1,0:T(8,128)S(1)} %get-tuple-element.32, f32[1,128,128]{2,1,0:T(8,128)S(1)} %get-tuple-element.33), kind=kOutput, calls=%fused_computation.9 | convolution fusion | flops 271155200 | bytes 3342464 | tf_op jit(solution)/shard_map/kux,pxkv->puv/dot_general | solution.py:59
  25.0 0.7 copy.36
  25.7 1.4 fusion
  27.5 0.6 copy.30
  28.1 15.2 %all-to-all-start = ((s32[16,2,2]{1,2,0:T(2,128)}), s32[16,2,2]{1,2,0:T(2,128)S(1)}, u32[]{:S(2)}, u32[]{:S(2)}) async-start(s32[16,2,2]{1,2,0:T(2,128)} %copy.30), calls=%async_computation | async-start | bytes 32768 | tf_op jit(solution)/shard_map/all_to_all | solution.py:95
  43.3 0.7 convolution_convert_fusion
  44.0 1.5 reshape.291
  45.5 10.4 %all-to-all-done = s32[16,2,2]{1,2,0:T(2,128)S(1)} async-done(((s32[16,2,2]{1,2,0:T(2,128)}), s32[16,2,2]{1,2,0:T(2,128)S(1)}, u32[]{:S(2)}, u32[]{:S(2)}) %all-to-all-start) | async-done | bytes 288 | tf_op jit(solution)/shard_map/all_to_all | solution.py:95
  55.9 3.7 %all-to-all-start.1 = ((bf16[16,2,16384]{2,1,0:T(2,128)(2,1)}), bf16[16,2,16384]{2,1,0:T(2,128)(2,1)S(1)}, u32[]{:S(2)}, u32[]{:S(2)}) async-start(bf16[16,2,16384]{2,1,0:T(2,128)(2,1)} %reshape.291), calls=%async_computation.1 | async-start | bytes 2097152 | tf_op jit(solution)/shard_map/all_to_all | solution.py:94
  60.1 82.0 %all-gather = s32[16,6,5]{2,1,0:T(8,128)S(1)} all-gather(s32[1,6,5]{2,1,0:T(8,128)S(1)} %bitcast.75), channel_id=1, replica_groups=mesh['dom'=32,'cls'=16] {'cls'}, dimensions={0}, use_global_device_ids=true | all-gather | bytes 2040 | tf_op jit(solution)/shard_map/all_gather | solution.py:120
  142.8 9.6 %fusion.8 = f32[16,16384]{1,0:T(8,128)} fusion(f32[16,32]{1,0:T(8,128)S(1)} %fusion.48, f32[16384]{0:T(1024)S(1)} %get-tuple-element.20, f32[32]{0:T(128)S(1)} %copy-done.3), kind=kOutput, calls=%fused_computation.12 | convolution fusion | flops 102236160 | bytes 1116288 | tf_op jit(solution)/shard_map/dot_general | solution.py:140
  152.4 0.4 reshape.292
  152.8 4.9 %reshape.296 = bf16[96,16384]{1,0:T(8,128)(2,1)} reshape(bf16[16,6,16384]{2,1,0:T(8,128)(2,1)} %all-gather.4.cloned.1.call-done) | data formatting | bytes 6291456
  157.7 3.5 %fusion.1 = f32[16,16384]{1,0:T(8,128)} fusion(bf16[96,16384]{1,0:T(8,128)(2,1)} %reshape.296, bf16[32,16384]{1,0:T(8,128)(2,1)S(1)} %reshape.292, s32[128]{0:T(128)S(1)} %get-tuple-element.17), kind=kOutput, calls=%fused_computation.4 | convolution fusion | flops 75499520 | bytes 5243392 | tf_op jit(solution)/shard_map/dot_general | solution.py:135
  161.3 136.9 %all-reduce.3.cloned.1.call-done = (f32[16,16384]{1,0:T(8,128)}, f32[16,16384]{1,0:T(8,128)}) async-done(((f32[16,16384]{1,0:T(8,128)}, f32[16,16384]{1,0:T(8,128)}), (f32[16,16384]{1,0:T(8,128)}, f32[16,16384]{1,0:T(8,128)})) %all-reduce.3.cloned.1.call-update) | async-done | bytes 2097168 | tf_op jit(solution)/shard_map/psum | solution.py:141
  298.1 1.7 divide_bitcast_fusion.1
  300.0 1.8 fusion.21
  301.9 1.9 multiply_reduce_fusion
  303.9 1.3 copy.38
  (48 shorter events, 3.3 us)
Async XLA Ops:
  6.5 2.4 copy-start
  6.5 146.3 %all-gather.4.cloned.1.call-start = ((), (), s32[]{:S(2)}) async-start(), calls=%async_computation.2 | async-start | bytes 4456448 | tf_op jit(solution)/shard_map/all_gather | solution.py:119
  13.3 2.3 copy-start.2
  13.3 2.3 copy-start.3
  28.1 27.8 %all-to-all-start = ((s32[16,2,2]{1,2,0:T(2,128)}), s32[16,2,2]{1,2,0:T(2,128)S(1)}, u32[]{:S(2)}, u32[]{:S(2)}) async-start(s32[16,2,2]{1,2,0:T(2,128)} %copy.30), calls=%async_computation | async-start | bytes 32768 | tf_op jit(solution)/shard_map/all_to_all | solution.py:95
  55.9 96.4 %all-to-all-start.1 = ((bf16[16,2,16384]{2,1,0:T(2,128)(2,1)}), bf16[16,2,16384]{2,1,0:T(2,128)(2,1)S(1)}, u32[]{:S(2)}, u32[]{:S(2)}) async-start(bf16[16,2,16384]{2,1,0:T(2,128)(2,1)} %reshape.291), calls=%async_computation.1 | async-start | bytes 2097152 | tf_op jit(solution)/shard_map/all_to_all | solution.py:94
  59.6 238.6 %all-reduce.3.cloned.1.call-start = ((), (), s32[]{:S(2)}) async-start(), calls=%async_computation.3 | async-start | bytes 4194304 | tf_op jit(solution)/shard_map/psum | solution.py:141
  161.2 136.9 %copy-start.1 = (f32[128,128]{1,0:T(8,128)S(1)}, f32[128,128]{1,0:T(8,128)}, u32[]{:S(2)}) copy-start(f32[128,128]{1,0:T(8,128)} %param.11) | copy-start | bytes 196612
Sparse Core Ops, SparseCore 0:
  27.2 124.3 all-gather.3
  161.4 136.7 all-reduce.2
where the time goes:
time: 313 us; the launch traced here: 312 us
  waiting for transfers between devices  147 us (47%)
  blocking collectives  82 us (26%)
  matrix products  32.6 us (10%)
  starting transfers between devices  18.9 us (6%)
  between operations  13.6 us (4%)
  local copies, waits for them, and re-layouts  13.3 us (4%)
  other arithmetic  4.4 us (1%)
    psum x1, waiting for transfers between devices, body(): numerator, denominator = lax.psum((numerator, denominator), 'dom')  137 us
    all_gather x1, blocking collectives, body(): lax.all_gather(extra_tags, 'cls', axis=0, tiled=True)  82 us
    all_to_all x1, starting transfers between devices, body(): lax.all_to_all(labels, 'cls', split_axis=0, concat_axis=0, tiled=True)  15.2 us
    all_to_all x1, waiting for transfers between devices, body(): lax.all_to_all(labels, 'cls', split_axis=0, concat_axis=0, tiled=True)  10.4 us
    dot_general x1, matrix products, body(): denominator = jnp.dot(counts, ctf_table, precision=lax.Precision.HIGHEST)  9.57 us
    dot_general x1, matrix products, weigh(): jnp.einsum('kux,pxkv->puv', left_table, halves, preferred_element_type=jn...  9.16 us
  transfers between devices with their start and end apart: 4, of which 2 were waited for; matrix products, arithmetic and copies ran while one was open for 5% of the time, Pallas kernels for 0%

commit v1 on v0

--- a/solution.py
+++ b/solution.py
@@ -1,3 +1,4 @@
+import functools
 import math
 import jax
 import jax.numpy as jnp
@@ -7,6 +8,32 @@
 OWNED = 16
 PHASE = 0.1
 EPSILON = 1e-05
+
+
+def side_arrange(content, axis_k):
+    w2, low, piece_out = (lax.axis_size("cls"), lax.axis_index("cls"), content.shape[axis_k])
+    store = [(it, (it + 1) % w2) for it in range(w2)]
+    w_next = jnp.zeros(
+        (*content.shape[:axis_k], w2 * piece_out, *content.shape[axis_k + 1 :]), content.dtype
+    )
+    w_next = lax.dynamic_update_slice_in_dim(w_next, content, low * piece_out, axis=axis_k)
+    passed = met_up = content
+    a_now = w2 // 2
+    views = [(it, (it - 1) % w2) for it in range(w2)]
+    for q in range(1, a_now + 1):
+        passed = lax.ppermute(passed, axis_name="cls", perm=store)
+        w_next = lax.dynamic_update_slice_in_dim(
+            w_next, passed, (low - q) % w2 * piece_out, axis=axis_k
+        )
+        if q < w2 - a_now:
+            met_up = lax.ppermute(met_up, axis_name="cls", perm=views)
+            w_next = lax.dynamic_update_slice_in_dim(
+                w_next, met_up, (low + q) % w2 * piece_out, axis=axis_k
+            )
+    return w_next
+
+
+_resolve_row = functools.partial(side_arrange, axis_k=0)
 
 
 def hartley_tables(image_side):
@@ -117,7 +144,7 @@
     )
     gathered_rows, gathered_tags = (
         lax.all_gather(extra_rows, "cls", axis=0, tiled=True),
-        lax.all_gather(extra_tags, "cls", axis=0, tiled=True),
+        _resolve_row(extra_tags),
     )
     mine = gathered_tags[:, 4] == lax.axis_index("cls")
     kept_class = jnp.where(mine, gathered_tags[:, 0], OWNED)

time: 313 us -> 341 us (1.089)
  blocking collectives: 82 us -> 0 us
  waiting for transfers between devices: 147 us -> 202 us
  starting transfers between devices: 18.9 us -> 70.3 us
  local copies, waits for them, and re-layouts: 13.3 us -> 16.9 us
    all_gather x1 -> x0, blocking collectives: 82 us -> none  [body(): lax.all_gather(extra_tags, 'cls', axis=0, tiled=True)]
    ppermute x0 -> x15, waiting for transfers between devices: none -> 53.2 us  [the longest x8 53.2 us: side_arrange(): passed = lax.ppermute(passed, axis_name='cls', perm=store)]
    ppermute x0 -> x15, starting transfers between devices: none -> 51.5 us  [the longest x7 32.7 us: side_arrange(): met_up = lax.ppermute(met_up, axis_name='cls', perm=views)]
    dynamic_update_slice x0 -> x16, local copies, waits for them, and re-layouts: none -> 4.07 us  [the longest x8 2.12 us: side_arrange(): lax.dynamic_update_slice_in_dim(w_next, passed, (low - q) % w2 * piece_ou...]
  transfers between devices with their start and end apart: 4 -> 19, of which waited for: 2 -> 4; matrix products, arithmetic and copies ran while one was open for 5% -> 5% of each run, Pallas kernels for 0% -> 0%
where the time goes in v1:
time: 341 us; the launch traced here: 340 us
  waiting for transfers between devices  202 us (59%)
  starting transfers between devices  70.3 us (21%)
  matrix products  32.6 us (10%)
  local copies, waits for them, and re-layouts  16.9 us (5%)
  between operations  14.2 us (4%)
  other arithmetic  3.75 us (1%)
    psum x1, waiting for transfers between devices, body(): numerator, denominator = lax.psum((numerator, denominator), 'dom')  139 us
    ppermute x8, waiting for transfers between devices, side_arrange(): passed = lax.ppermute(passed, axis_name='cls', perm=store)  53.2 us
    ppermute x7, starting transfers between devices, side_arrange(): met_up = lax.ppermute(met_up, axis_name='cls', perm=views)  32.7 us
    ppermute x8, starting transfers between devices, side_arrange(): passed = lax.ppermute(passed, axis_name='cls', perm=store)  18.8 us
    all_to_all x1, starting transfers between devices, body(): lax.all_to_all(labels, 'cls', split_axis=0, concat_axis=0, tiled=True)  15.2 us
    all_to_all x1, waiting for transfers between devices, body(): lax.all_to_all(labels, 'cls', split_axis=0, concat_axis=0, tiled=True)  10.4 us
    dot_general x1, matrix products, body(): denominator = jnp.dot(counts, ctf_table, precision=lax.Precision.HIGHEST)  9.56 us
    dot_general x1, matrix products, weigh(): jnp.einsum('kux,pxkv->puv', left_table, halves, preferred_element_type=jn...  9.16 us
  transfers between devices with their start and end apart: 19, of which 4 were waited for; matrix products, arithmetic and copies ran while one was open for 5% of the time, Pallas kernels for 0%

profile of v1, /device:TPU:6, one launch (start us, length us, event | category | flops | bytes accessed | tf_op | source)
XLA Modules:
  0.0 340.3 jit_solution(14037906753523479011)
XLA Ops:
  8.0 2.4 fusion.15
  10.4 1.9 convolution_convert_fusion.2
  12.4 2.1 reshape.289
  14.8 9.2 %fusion.5 = bf16[32,128,128]{1,2,0:T(8,128)(2,1)S(1)} fusion(bf16[32,128,2,128]{3,2,1,0:T(2,128)(2,1)} %reshape.289, f32[128,128]{0,1:T(8,128)S(1)} %copy.24, f32[32]{0:T(128)S(1)} %select_reduce_fusion, f32[1,128,128]{2,1,0:T(8,128)S(1)} %get-tuple-element.32, f32[1,128,128]{2,1,0:T(8,128)S(1)} %get-tuple-element.33), kind=kOutput, calls=%fused_computation.9 | convolution fusion | flops 271155200 | bytes 3342464 | tf_op jit(solution)/shard_map/kux,pxkv->puv/dot_general | solution.py:86
  27.5 15.2 %all-to-all-start = ((s32[16,2,2]{1,2,0:T(2,128)}), s32[16,2,2]{1,2,0:T(2,128)S(1)}, u32[]{:S(2)}, u32[]{:S(2)}) async-start(s32[16,2,2]{1,2,0:T(2,128)} %copy.22), calls=%async_computation | async-start | bytes 32768 | tf_op jit(solution)/shard_map/all_to_all | solution.py:122
  44.9 10.4 %all-to-all-done = s32[16,2,2]{1,2,0:T(2,128)S(1)} async-done(((s32[16,2,2]{1,2,0:T(2,128)}), s32[16,2,2]{1,2,0:T(2,128)S(1)}, u32[]{:S(2)}, u32[]{:S(2)}) %all-to-all-start) | async-done | bytes 288 | tf_op jit(solution)/shard_map/all_to_all | solution.py:122
  55.3 3.7 %all-to-all-start.1 = ((bf16[16,2,16384]{2,1,0:T(2,128)(2,1)}), bf16[16,2,16384]{2,1,0:T(2,128)(2,1)S(1)}, u32[]{:S(2)}, u32[]{:S(2)}) async-start(bf16[16,2,16384]{2,1,0:T(2,128)(2,1)} %reshape.291), calls=%async_computation.1 | async-start | bytes 2097152 | tf_op jit(solution)/shard_map/all_to_all | solution.py:121
  59.3 3.7 %collective-permute-start = (s32[6,5]{0,1:T(8,128)S(1)}, s32[6,5]{0,1:T(8,128)S(1)}, u32[]{:S(2)}, u32[]{:S(2)}) collective-permute-start(s32[6,5]{0,1:T(8,128)S(1)} %stack.41), channel_id=1, source_target_pairs={{0,1},{1,2},{2,3},{3,4},{4,5},{5,6},{6,7},{7,8},{8,9},{9,10},{10,1... | collective-permute-start | bytes 368 | tf_op jit(solution)/shard_map/ppermute | solution.py:24
  63.1 3.3 collective-permute-start.1
  67.0 49.1 %collective-permute-done = s32[6,5]{0,1:T(8,128)S(1)} collective-permute-done((s32[6,5]{0,1:T(8,128)S(1)}, s32[6,5]{0,1:T(8,128)S(1)}, u32[]{:S(2)}, u32[]{:S(2)}) %collective-permute-start) | collective-permute-done | bytes 152 | tf_op jit(solution)/shard_map/ppermute | solution.py:24
  116.1 3.3 collective-permute-start.2
  119.4 3.7 %collective-permute-start.3 = (s32[6,5]{0,1:T(8,128)S(1)}, s32[6,5]{0,1:T(8,128)S(1)}, u32[]{:S(2)}, u32[]{:S(2)}) collective-permute-start(s32[6,5]{0,1:T(8,128)S(1)} %collective-permute-done.1), channel_id=1, source_target_pairs={{0,15},{1,0},{2,1},{3,2},{4,3},{5,4},{6,5},{7,6},{8,7},{9,8},{10,9... | collective-permute-start | bytes 368 | tf_op jit(solution)/shard_map/ppermute | solution.py:29
  123.7 2.1 collective-permute-start.4
  125.8 4.9 %collective-permute-start.5 = (s32[6,5]{0,1:T(8,128)S(1)}, s32[6,5]{0,1:T(8,128)S(1)}, u32[]{:S(2)}, u32[]{:S(2)}) collective-permute-start(s32[6,5]{0,1:T(8,128)S(1)} %collective-permute-done.3), channel_id=1, source_target_pairs={{0,15},{1,0},{2,1},{3,2},{4,3},{5,4},{6,5},{7,6},{8,7},{9,8},{10,9... | collective-permute-start | bytes 368 | tf_op jit(solution)/shard_map/ppermute | solution.py:29
  133.2 5.1 %collective-permute-start.7 = (s32[6,5]{0,1:T(8,128)S(1)}, s32[6,5]{0,1:T(8,128)S(1)}, u32[]{:S(2)}, u32[]{:S(2)}) collective-permute-start(s32[6,5]{0,1:T(8,128)S(1)} %collective-permute-done.5), channel_id=1, source_target_pairs={{0,15},{1,0},{2,1},{3,2},{4,3},{5,4},{6,5},{7,6},{8,7},{9,8},{10,9... | collective-permute-start | bytes 368 | tf_op jit(solution)/shard_map/ppermute | solution.py:29
  140.8 5.1 %collective-permute-start.9 = (s32[6,5]{0,1:T(8,128)S(1)}, s32[6,5]{0,1:T(8,128)S(1)}, u32[]{:S(2)}, u32[]{:S(2)}) collective-permute-start(s32[6,5]{0,1:T(8,128)S(1)} %collective-permute-done.7), channel_id=1, source_target_pairs={{0,15},{1,0},{2,1},{3,2},{4,3},{5,4},{6,5},{7,6},{8,7},{9,8},{10,9... | collective-permute-start | bytes 368 | tf_op jit(solution)/shard_map/ppermute | solution.py:29
  148.4 5.1 %collective-permute-start.11 = (s32[6,5]{0,1:T(8,128)S(1)}, s32[6,5]{0,1:T(8,128)S(1)}, u32[]{:S(2)}, u32[]{:S(2)}) collective-permute-start(s32[6,5]{0,1:T(8,128)S(1)} %collective-permute-done.9), channel_id=1, source_target_pairs={{0,15},{1,0},{2,1},{3,2},{4,3},{5,4},{6,5},{7,6},{8,7},{9,8},{10,9... | collective-permute-start | bytes 368 | tf_op jit(solution)/shard_map/ppermute | solution.py:29
  154.1 1.9 collective-permute-start.12
  156.0 5.3 %collective-permute-start.13 = (s32[6,5]{0,1:T(8,128)S(1)}, s32[6,5]{0,1:T(8,128)S(1)}, u32[]{:S(2)}, u32[]{:S(2)}) collective-permute-start(s32[6,5]{0,1:T(8,128)S(1)} %collective-permute-done.11), channel_id=1, source_target_pairs={{0,15},{1,0},{2,1},{3,2},{4,3},{5,4},{6,5},{7,6},{8,7},{9,8},{10,9... | collective-permute-start | bytes 368 | tf_op jit(solution)/shard_map/ppermute | solution.py:29
  164.5 4.1 %collective-permute-done.14 = s32[6,5]{0,1:T(8,128)S(1)} collective-permute-done((s32[6,5]{0,1:T(8,128)S(1)}, s32[6,5]{0,1:T(8,128)S(1)}, u32[]{:S(2)}, u32[]{:S(2)}) %collective-permute-start.14) | collective-permute-done | bytes 152 | tf_op jit(solution)/shard_map/ppermute | solution.py:24
  169.1 9.6 %fusion.8 = f32[16,16384]{1,0:T(8,128)} fusion(f32[16,32]{1,0:T(8,128)S(1)} %fusion.48, f32[16384]{0:T(1024)S(1)} %get-tuple-element.20, f32[32]{0:T(128)S(1)} %copy-done.4), kind=kOutput, calls=%fused_computation.12 | convolution fusion | flops 102236160 | bytes 1116288 | tf_op jit(solution)/shard_map/dot_general | solution.py:167
  179.1 4.9 %reshape.294 = bf16[96,16384]{1,0:T(8,128)(2,1)} reshape(bf16[16,6,16384]{2,1,0:T(8,128)(2,1)} %all-gather.3.cloned.1.call-done) | data formatting | bytes 6291456
  184.0 3.5 %fusion.1 = f32[16,16384]{1,0:T(8,128)} fusion(bf16[96,16384]{1,0:T(8,128)(2,1)} %reshape.294, bf16[32,16384]{1,0:T(8,128)(2,1)S(1)} %reshape.292, s32[128]{0:T(128)S(1)} %get-tuple-element.17), kind=kOutput, calls=%fused_computation.4 | convolution fusion | flops 75499520 | bytes 5243392 | tf_op jit(solution)/shard_map/dot_general | solution.py:162
  187.6 138.8 %all-reduce.3.cloned.1.call-done = (f32[16,16384]{1,0:T(8,128)}, f32[16,16384]{1,0:T(8,128)}) async-done(((f32[16,16384]{1,0:T(8,128)}, f32[16,16384]{1,0:T(8,128)}), (f32[16,16384]{1,0:T(8,128)}, f32[16,16384]{1,0:T(8,128)})) %all-reduce.3.cloned.1.call-update) | async-done | bytes 2097168 | tf_op jit(solution)/shard_map/psum | solution.py:168
  (93 shorter events, 27.5 us)
Async XLA Ops:
  6.5 1.4 copy-start
  6.5 172.5 %all-gather.3.cloned.1.call-start = ((), (), s32[]{:S(2)}) async-start(), calls=%async_computation.2 | async-start | bytes 4456448 | tf_op jit(solution)/shard_map/all_gather | solution.py:146
  12.4 2.3 copy-start.2
  12.4 2.3 copy-start.4
  24.0 0.7 copy-start.3
  27.5 27.8 %all-to-all-start = ((s32[16,2,2]{1,2,0:T(2,128)}), s32[16,2,2]{1,2,0:T(2,128)S(1)}, u32[]{:S(2)}, u32[]{:S(2)}) async-start(s32[16,2,2]{1,2,0:T(2,128)} %copy.22), calls=%async_computation | async-start | bytes 32768 | tf_op jit(solution)/shard_map/all_to_all | solution.py:122
  55.3 123.3 %all-to-all-start.1 = ((bf16[16,2,16384]{2,1,0:T(2,128)(2,1)}), bf16[16,2,16384]{2,1,0:T(2,128)(2,1)S(1)}, u32[]{:S(2)}, u32[]{:S(2)}) async-start(bf16[16,2,16384]{2,1,0:T(2,128)(2,1)} %reshape.291), calls=%async_computation.1 | async-start | bytes 2097152 | tf_op jit(solution)/shard_map/all_to_all | solution.py:121
  59.0 267.4 %all-reduce.3.cloned.1.call-start = ((), (), s32[]{:S(2)}) async-start(), calls=%async_computation.3 | async-start | bytes 4194304 | tf_op jit(solution)/shard_map/psum | solution.py:168
  59.3 56.7 %collective-permute-start = (s32[6,5]{0,1:T(8,128)S(1)}, s32[6,5]{0,1:T(8,128)S(1)}, u32[]{:S(2)}, u32[]{:S(2)}) collective-permute-start(s32[6,5]{0,1:T(8,128)S(1)} %stack.41), channel_id=1, source_target_pairs={{0,1},{1,2},{2,3},{3,4},{4,5},{5,6},{6,7},{7,8},{8,9},{9,10},{10,1... | collective-permute-start | bytes 368 | tf_op jit(solution)/shard_map/ppermute | solution.py:24
  63.1 56.4 %collective-permute-start.1 = (s32[6,5]{0,1:T(8,128)S(1)}, s32[6,5]{0,1:T(8,128)S(1)}, u32[]{:S(2)}, u32[]{:S(2)}) collective-permute-start(s32[6,5]{0,1:T(8,128)S(1)} %stack.41), channel_id=1, source_target_pairs={{0,15},{1,0},{2,1},{3,2},{4,3},{5,4},{6,5},{7,6},{8,7},{9,8},{10,9... | collective-permute-start | bytes 368 | tf_op jit(solution)/shard_map/ppermute | solution.py:29
  116.1 7.6 %collective-permute-start.2 = (s32[6,5]{0,1:T(8,128)S(1)}, s32[6,5]{0,1:T(8,128)S(1)}, u32[]{:S(2)}, u32[]{:S(2)}) collective-permute-start(s32[6,5]{0,1:T(8,128)S(1)} %collective-permute-done), channel_id=1, source_target_pairs={{0,1},{1,2},{2,3},{3,4},{4,5},{5,6},{6,7},{7,8},{8,9},{9,10},{10,1... | collective-permute-start | bytes 368 | tf_op jit(solution)/shard_map/ppermute | solution.py:24
  119.4 6.4 %collective-permute-start.3 = (s32[6,5]{0,1:T(8,128)S(1)}, s32[6,5]{0,1:T(8,128)S(1)}, u32[]{:S(2)}, u32[]{:S(2)}) collective-permute-start(s32[6,5]{0,1:T(8,128)S(1)} %collective-permute-done.1), channel_id=1, source_target_pairs={{0,15},{1,0},{2,1},{3,2},{4,3},{5,4},{6,5},{7,6},{8,7},{9,8},{10,9... | collective-permute-start | bytes 368 | tf_op jit(solution)/shard_map/ppermute | solution.py:29
  123.7 7.6 %collective-permute-start.4 = (s32[6,5]{0,1:T(8,128)S(1)}, s32[6,5]{0,1:T(8,128)S(1)}, u32[]{:S(2)}, u32[]{:S(2)}) collective-permute-start(s32[6,5]{0,1:T(8,128)S(1)} %collective-permute-done.2), channel_id=1, source_target_pairs={{0,1},{1,2},{2,3},{3,4},{4,5},{5,6},{6,7},{7,8},{8,9},{9,10},{10,1... | collective-permute-start | bytes 368 | tf_op jit(solution)/shard_map/ppermute | solution.py:24
  125.8 7.4 %collective-permute-start.5 = (s32[6,5]{0,1:T(8,128)S(1)}, s32[6,5]{0,1:T(8,128)S(1)}, u32[]{:S(2)}, u32[]{:S(2)}) collective-permute-start(s32[6,5]{0,1:T(8,128)S(1)} %collective-permute-done.3), channel_id=1, source_target_pairs={{0,15},{1,0},{2,1},{3,2},{4,3},{5,4},{6,5},{7,6},{8,7},{9,8},{10,9... | collective-permute-start | bytes 368 | tf_op jit(solution)/shard_map/ppermute | solution.py:29
  131.3 7.6 %collective-permute-start.6 = (s32[6,5]{0,1:T(8,128)S(1)}, s32[6,5]{0,1:T(8,128)S(1)}, u32[]{:S(2)}, u32[]{:S(2)}) collective-permute-start(s32[6,5]{0,1:T(8,128)S(1)} %collective-permute-done.4), channel_id=1, source_target_pairs={{0,1},{1,2},{2,3},{3,4},{4,5},{5,6},{6,7},{7,8},{8,9},{9,10},{10,1... | collective-permute-start | bytes 368 | tf_op jit(solution)/shard_map/ppermute | solution.py:24
  133.2 7.6 %collective-permute-start.7 = (s32[6,5]{0,1:T(8,128)S(1)}, s32[6,5]{0,1:T(8,128)S(1)}, u32[]{:S(2)}, u32[]{:S(2)}) collective-permute-start(s32[6,5]{0,1:T(8,128)S(1)} %collective-permute-done.5), channel_id=1, source_target_pairs={{0,15},{1,0},{2,1},{3,2},{4,3},{5,4},{6,5},{7,6},{8,7},{9,8},{10,9... | collective-permute-start | bytes 368 | tf_op jit(solution)/shard_map/ppermute | solution.py:29
  138.9 7.6 %collective-permute-start.8 = (s32[6,5]{0,1:T(8,128)S(1)}, s32[6,5]{0,1:T(8,128)S(1)}, u32[]{:S(2)}, u32[]{:S(2)}) collective-permute-start(s32[6,5]{0,1:T(8,128)S(1)} %collective-permute-done.6), channel_id=1, source_target_pairs={{0,1},{1,2},{2,3},{3,4},{4,5},{5,6},{6,7},{7,8},{8,9},{9,10},{10,1... | collective-permute-start | bytes 368 | tf_op jit(solution)/shard_map/ppermute | solution.py:24
  140.8 7.6 %collective-permute-start.9 = (s32[6,5]{0,1:T(8,128)S(1)}, s32[6,5]{0,1:T(8,128)S(1)}, u32[]{:S(2)}, u32[]{:S(2)}) collective-permute-start(s32[6,5]{0,1:T(8,128)S(1)} %collective-permute-done.7), channel_id=1, source_target_pairs={{0,15},{1,0},{2,1},{3,2},{4,3},{5,4},{6,5},{7,6},{8,7},{9,8},{10,9... | collective-permute-start | bytes 368 | tf_op jit(solution)/shard_map/ppermute | solution.py:29
  146.5 7.6 %collective-permute-start.10 = (s32[6,5]{0,1:T(8,128)S(1)}, s32[6,5]{0,1:T(8,128)S(1)}, u32[]{:S(2)}, u32[]{:S(2)}) collective-permute-start(s32[6,5]{0,1:T(8,128)S(1)} %collective-permute-done.8), channel_id=1, source_target_pairs={{0,1},{1,2},{2,3},{3,4},{4,5},{5,6},{6,7},{7,8},{8,9},{9,10},{10,1... | collective-permute-start | bytes 368 | tf_op jit(solution)/shard_map/ppermute | solution.py:24
  148.4 7.6 %collective-permute-start.11 = (s32[6,5]{0,1:T(8,128)S(1)}, s32[6,5]{0,1:T(8,128)S(1)}, u32[]{:S(2)}, u32[]{:S(2)}) collective-permute-start(s32[6,5]{0,1:T(8,128)S(1)} %collective-permute-done.9), channel_id=1, source_target_pairs={{0,15},{1,0},{2,1},{3,2},{4,3},{5,4},{6,5},{7,6},{8,7},{9,8},{10,9... | collective-permute-start | bytes 368 | tf_op jit(solution)/shard_map/ppermute | solution.py:29
  154.1 7.8 %collective-permute-start.12 = (s32[6,5]{0,1:T(8,128)S(1)}, s32[6,5]{0,1:T(8,128)S(1)}, u32[]{:S(2)}, u32[]{:S(2)}) collective-permute-start(s32[6,5]{0,1:T(8,128)S(1)} %collective-permute-done.10), channel_id=1, source_target_pairs={{0,1},{1,2},{2,3},{3,4},{4,5},{5,6},{6,7},{7,8},{8,9},{9,10},{10,1... | collective-permute-start | bytes 368 | tf_op jit(solution)/shard_map/ppermute | solution.py:24
  156.0 8.1 %collective-permute-start.13 = (s32[6,5]{0,1:T(8,128)S(1)}, s32[6,5]{0,1:T(8,128)S(1)}, u32[]{:S(2)}, u32[]{:S(2)}) collective-permute-start(s32[6,5]{0,1:T(8,128)S(1)} %collective-permute-done.11), channel_id=1, source_target_pairs={{0,15},{1,0},{2,1},{3,2},{4,3},{5,4},{6,5},{7,6},{8,7},{9,8},{10,9... | collective-permute-start | bytes 368 | tf_op jit(solution)/shard_map/ppermute | solution.py:29
  161.9 6.7 %collective-permute-start.14 = (s32[6,5]{0,1:T(8,128)S(1)}, s32[6,5]{0,1:T(8,128)S(1)}, u32[]{:S(2)}, u32[]{:S(2)}) collective-permute-start(s32[6,5]{0,1:T(8,128)S(1)} %collective-permute-done.12), channel_id=1, source_target_pairs={{0,1},{1,2},{2,3},{3,4},{4,5},{5,6},{6,7},{7,8},{8,9},{9,10},{10,1... | collective-permute-start | bytes 368 | tf_op jit(solution)/shard_map/ppermute | solution.py:24
  187.5 138.8 %copy-start.1 = (f32[128,128]{1,0:T(8,128)S(1)}, f32[128,128]{1,0:T(8,128)}, u32[]{:S(2)}) copy-start(f32[128,128]{1,0:T(8,128)} %param.11) | copy-start | bytes 196612
Sparse Core Ops, SparseCore 0:
  26.6 124.3 all-gather.2
  187.7 138.6 all-reduce.2
